TPU v7x, 768 devices: a whole 4x8x12 slice. The times are simulated.
768 devices in a mesh: row: 48 (over z, x_hi, core), col: 16 (over y, x_lo).
Axes of the slice: x: 4 (x_hi: 2, x_lo: 2; x = x_hi * 2 + x_lo), y: 8, z: 12, core: 2. Of those that a mesh axis runs over, the one named last changes fastest.
Arguments:
- vectors: bfloat16 [8, 196608], P(None, ('row', 'col')), may hold values from -6 to 6
- blocks: bfloat16 [48, 16, 32, 128, 128], P('row', 'col'), may hold values from -0.0625 to 0.0625
- row_index: int32 [48, 16, 32], P('row', 'col'), may hold values from 0 to 31, as said below
- col_index: int32 [48, 16, 32], P('row', 'col'), may hold values from 0 to 95
- live: int32 [48, 16], P('row', 'col'), may hold values from 1 to 32, as said below
Outputs:
- applied: float32 [8, 196608], P(None, ('row', 'col'))
Inputs may be any that keep to these rules, and one draw needn't show every extreme that they name: row_index lies in 0 to 31 and col_index in 0 to 95; live slots are the first live[i, j] of their cell, each lies on or above the block diagonal, and no pair repeats within a cell. Some cell holds 32 live slots in every draw.
All inputs are finite; a program needn't handle non-finite values.
Results may differ from a plain program's by a relative error of at most 0.0003.
Values may be sent and summed in bfloat16 or wider, within the bound.
A program may use at most 32 MiB of HBM per device.

v0:
```python
import jax
import jax.numpy as jnp
from jax import lax
from jax.sharding import PartitionSpec as P


def pick_blocks(states, indices, width):
    count = states.shape[1] // width
    tiled = states.reshape(states.shape[0], count, width)
    return jnp.take(tiled, indices, axis=1)


def place_blocks(terms, indices, count):
    one_hot = (indices[:, None] == jnp.arange(count, dtype=jnp.int32)[None, :]).astype(jnp.float32)
    placed = jnp.einsum("kr,vki->vri", one_hot, terms, precision=lax.Precision.HIGHEST)
    return placed.reshape(terms.shape[0], count * terms.shape[2])


def local(vectors, blocks, row_index, col_index, live):
    n_row = lax.axis_size("row")
    n_col = lax.axis_size("col")
    piece = vectors.shape[1]
    width = blocks.shape[-1]
    nvec = vectors.shape[0]
    every = lax.all_gather(vectors, ("row", "col"), axis=1, tiled=True)
    grid = every.reshape(nvec, n_row, n_col, piece)
    row_states = lax.dynamic_index_in_dim(grid, lax.axis_index("row"), 1, keepdims=False).reshape(
        nvec, n_col * piece
    )
    col_states = lax.dynamic_index_in_dim(grid, lax.axis_index("col"), 2, keepdims=False).reshape(
        nvec, n_row * piece
    )
    stored = blocks.reshape(blocks.shape[2], width, width)
    row_ids = row_index.reshape(-1)
    col_ids = col_index.reshape(-1)
    mask = (jnp.arange(stored.shape[0], dtype=jnp.int32) < live.reshape(())).astype(jnp.float32)
    from_cols = pick_blocks(col_states, col_ids, width)
    from_rows = pick_blocks(row_states, row_ids, width)
    upper = jnp.einsum("kij,vkj->vki", stored, from_cols, preferred_element_type=jnp.float32)
    lower = jnp.einsum("kij,vki->vkj", stored, from_rows, preferred_element_type=jnp.float32)
    upper = upper * mask[None, :, None]
    lower = lower * mask[None, :, None]
    upper_part = place_blocks(upper, row_ids, n_col * piece // width)
    lower_part = place_blocks(lower, col_ids, n_row * piece // width)
    upper_mine = lax.psum_scatter(upper_part, "col", scatter_dimension=1, tiled=True)
    lower_mine = lax.psum_scatter(lower_part, "row", scatter_dimension=1, tiled=True)
    return upper_mine + lower_mine


def solution(mesh):
    return jax.shard_map(
        local,
        mesh=mesh,
        in_specs=(
            P(None, ("row", "col")),
            P("row", "col", None, None, None),
            P("row", "col", None),
            P("row", "col", None),
            P("row", "col"),
        ),
        out_specs=P(None, ("row", "col")),
        check_vma=False,
    )
```

profile of v0, /device:TPU:1, one launch (start us, length us, event | category | flops | bytes accessed | tf_op | source)
XLA Modules:
  0.0 1848.2 jit_solution(9807794157007812804)
XLA Ops:
  6.5 0.0 copy-start
  6.5 0.7 all-gather.2.cloned.1.call-update
  7.3 0.0 reduce-scatter.3.cloned.1.call-start
  8.0 0.7 fusion.22
  8.6 0.7 fusion.23
  9.3 0.7 compare_and_fusion.1
  10.0 0.7 compare_and_fusion
  10.6 1585.3 %all-gather.2.cloned.1.call-done = bf16[8,196608]{1,0:T(8,128)(2,1)} async-done(((bf16[8,256]{1,0:T(8,128)(2,1)}), bf16[8,196608]{1,0:T(8,128)(2,1)}) %all-gather.2.cloned.1.call-update) | async-done | bytes 3145744 | tf_op jit(solution)/shard_map/all_gather | solution.py:25
  1595.9 0.9 constant_dynamic-slice_fusion.1
  1596.9 0.6 gather_fusion
  1597.5 0.7 fusion.2
  1598.1 1.0 convolution_bitcast_fusion.1
  1599.1 0.7 copy.27
  1599.8 0.0 reduce-scatter.3.cloned.1.call-update
  1599.9 0.0 reduce-scatter.5.cloned.1.call-start
  1599.9 0.9 constant_dynamic-slice_fusion
  1600.8 0.6 gather_fusion.1
  1601.4 0.4 fusion
  1601.8 0.4 convolution_bitcast_fusion
  1602.2 1.0 copy.26
  1603.2 0.0 reduce-scatter.5.cloned.1.call-update
  1603.2 57.9 %reduce-scatter.3.cloned.1.call-done = f32[8,256]{1,0:T(8,128)} async-done(((f32[8,4096]{1,0:T(8,128)}), f32[8,256]{1,0:T(8,128)}) %reduce-scatter.3.cloned.1.call-update) | async-done | bytes 8208 | tf_op jit(solution)/shard_map/reduce_scatter | solution.py:45
  1661.2 179.2 %reduce-scatter.5.cloned.1.call-done = f32[8,256]{1,0:T(8,128)} async-done(((f32[8,12288]{1,0:T(8,128)}), f32[8,256]{1,0:T(8,128)}) %reduce-scatter.5.cloned.1.call-update) | async-done | bytes 8208 | tf_op jit(solution)/shard_map/reduce_scatter | solution.py:46
  1840.4 1.3 add.67
  (7 shorter events, 0.0 us)
Async XLA Ops:
  6.5 1590.9 %copy-start = (bf16[1,1,32,128,128]{4,3,2,1,0:T(8,128)(2,1)S(1)}, bf16[1,1,32,128,128]{4,3,2,1,0:T(8,128)(2,1)}, u32[]{:S(2)}) copy-start(bf16[1,1,32,128,128]{4,3,2,1,0:T(8,128)(2,1)} %param.6) | copy-start | bytes 3145732
  6.5 1595.3 %copy-start.1 = (s32[1,1,32]{2,1,0:T(1,128)S(1)}, s32[1,1,32]{2,1,0:T(1,128)}, u32[]{:S(2)}) copy-start(s32[1,1,32]{2,1,0:T(1,128)} %param.8) | copy-start | bytes 388
  6.5 1589.4 %all-gather.2.cloned.1.call-start = ((), (), s32[]{:S(2)}) async-start(), calls=%async_computation.2 | async-start | bytes 3149824 | tf_op jit(solution)/shard_map/all_gather | solution.py:25
  7.3 1653.9 %reduce-scatter.3.cloned.1.call-start = ((), (), s32[]{:S(2)}) async-start(), calls=%async_computation.3 | async-start | bytes 139264 | tf_op jit(solution)/shard_map/reduce_scatter | solution.py:45
  1599.9 240.5 %reduce-scatter.5.cloned.1.call-start = ((), (), s32[]{:S(2)}) async-start(), calls=%async_computation.4 | async-start | bytes 401408 | tf_op jit(solution)/shard_map/reduce_scatter | solution.py:46
Sparse Core Ops, SparseCore 0:
  9.9 1585.9 all-gather.1
  1600.0 61.1 reduce-scatter.2
  1667.1 173.2 reduce-scatter.4
where the time goes:
time: 1860 us; the launch traced here: 1850 us
  waiting for transfers between devices  1820 us (98%)
    all_gather x1, waiting for transfers between devices, local(): every = lax.all_gather(vectors, ('row', 'col'), axis=1, tiled=True)  1590 us
    reduce_scatter x1, waiting for transfers between devices, local(): lax.psum_scatter(lower_part, 'row', scatter_dimension=1, tiled=True)  179 us
    reduce_scatter x1, waiting for transfers between devices, local(): lax.psum_scatter(upper_part, 'col', scatter_dimension=1, tiled=True)  57.9 us
  transfers between devices with their start and end apart: 3, of which 3 were waited for; matrix products, arithmetic and copies ran while one was open for 0% of the time, Pallas kernels for 0%

commit v1 on v0

v1 whole, which is shorter than its diff:
```python
import functools

import jax
import jax.numpy as jnp
from jax import lax
from jax.experimental import pallas as pl
from jax.experimental.pallas import tpu as pltpu
from jax.sharding import PartitionSpec as P

MESH = pl.DeviceIdType.MESH
BF16 = jnp.bfloat16
F32 = jnp.float32


def iota(shape, dim):
    return lax.broadcasted_iota(jnp.int32, shape, dim)


def split_dot(one_hot, terms):
    high = terms.astype(BF16)
    low = (terms - high.astype(F32)).astype(BF16)
    return jnp.dot(one_hot, high, preferred_element_type=F32) + jnp.dot(one_hot, low, preferred_element_type=F32)


def loop(first, last, body):
    def step(index, carry):
        body(index)
        return carry

    lax.fori_loop(first, last, step, 0)


def kernel(
    n_chip, n_col, vec_hbm, blocks, row_hbm, col_hbm, live_hbm, out,
    vec, row_index, col_index, live, held, row_st, col_st, row_pick, col_pick, row_place, col_place,
    picked, terms, low, low_sib, low_in, up, up_in,
    fetch_sem, row_send, row_recv, col_send, col_recv, low_send, low_recv, up_send, up_recv, sib_send, sib_recv,
    sib_ready,
):
    slots, width = held.shape[0], held.shape[1]
    nvec = vec.shape[0]
    piece = 2 * nvec
    rows = slots * nvec
    n_y = n_col // 2
    row, col = lax.axis_index("row"), lax.axis_index("col")
    chip, core = row // 2, row % 2
    sibling = {"row": row + 1 - 2 * core, "col": col}

    turn = jnp.where(row == 0, 1, 0)

    def col_of(rank):
        place = (rank + turn) % n_col
        key = place // 2
        y = jnp.where(key % 2 == 0, key // 2, n_y - (key + 1) // 2)
        return y * 2 + place % 2

    y = col // 2
    key = jnp.where(2 * y < n_y + n_y % 2, 2 * y, 2 * (n_y - y) - 1)
    rank = (key * 2 + col % 2 - turn + n_col) % n_col

    fetches = [
        pltpu.make_async_copy(source, target, fetch_sem.at[index])
        for index, (source, target) in enumerate(
            ((vec_hbm, vec), (row_hbm, row_index), (col_hbm, col_index), (live_hbm, live), (blocks.at[0, 0], held))
        )
    ]
    for fetch in fetches:
        fetch.start()

    def pieces(slot):
        return pl.ds(pl.multiple_of(slot * piece, piece), piece)

    col_st[...] = jnp.zeros_like(col_st)
    mine = core * n_chip + chip

    barrier = pltpu.get_barrier_semaphore()

    def greet(device):
        pl.semaphore_signal(barrier, inc=1, device_id=device, device_id_type=MESH)

    loop(rank + 1, n_col, lambda r: greet({"row": row, "col": col_of(r)}))
    loop(chip + 1, n_chip, lambda q: greet({"row": q * 2 + core, "col": col}))

    @pl.when(core == 1)
    def _():
        greet(sibling)

    fetches[0].wait()
    own = vec[...].astype(F32)
    own = jnp.concatenate([own[:, :width], own[:, width:]], axis=0).astype(BF16)
    col_st[pieces(mine)] = own
    row_st[pieces(col)] = own

    earlier = rank + chip + 1 - core

    @pl.when(earlier > 0)
    def _():
        pl.semaphore_wait(barrier, earlier)

    @pl.when(core == 0)
    def _():
        pl.semaphore_signal(sib_ready, inc=1, device_id=sibling, device_id_type=MESH)

    def col_copy(source, target):
        place = pieces(core * n_chip + source)
        return pltpu.make_async_remote_copy(
            col_st.at[place], col_st.at[place], col_send.at[target], col_recv.at[source],
            device_id={"row": target * 2 + core, "col": col}, device_id_type=MESH,
        )

    def row_copy(source, target):
        return pltpu.make_async_remote_copy(
            row_st.at[pieces(source)], row_st.at[pieces(source)], row_send.at[target], row_recv.at[source],
            device_id={"row": row, "col": target}, device_id_type=MESH,
        )

    loop(0, chip, lambda q: col_copy(chip, q).start())
    loop(0, rank, lambda r: row_copy(col, col_of(r)).start())

    for fetch in fetches[1:4]:
        fetch.wait()
    alive = iota((1, slots), 1) < live[...]
    row_ids = jnp.where(alive, row_index[0], -1).astype(F32)
    col_ids = jnp.where(alive, col_index[0], -1).astype(F32)
    spread = (iota((slots, rows), 1) // nvec == iota((slots, rows), 0)).astype(F32).astype(BF16)
    spread_t = (iota((rows, slots), 0) // nvec == iota((rows, slots), 1)).astype(F32)

    def row_target(ids, vector):
        return jnp.where(ids < 0, -1, ids * nvec + vector)

    def col_target(ids, vector):
        place = (ids // 2) % 2 * n_chip + ids // 4
        return jnp.where(ids < 0, -1, place * piece + ids % 2 * nvec + vector)

    for ids, target, pick, place in (
        (row_ids, row_target, row_pick, row_place),
        (col_ids, col_target, col_pick, col_place),
    ):
        count = place.shape[0]
        lane = jnp.dot(ids.astype(BF16), spread, preferred_element_type=F32).astype(jnp.int32)
        lane = target(lane, iota((1, rows), 1) % nvec)
        place[...] = (iota((count, rows), 0) == lane).astype(F32).astype(BF16)
        line = jnp.sum(spread_t * ids, axis=1, keepdims=True).astype(jnp.int32)
        line = target(line, iota((rows, 1), 0) % nvec)
        pick[...] = (iota((rows, count), 1) == line).astype(F32).astype(BF16)

    def answer(r):
        other = col_of(r)
        row_copy(other, col).wait_recv()
        row_copy(col, other).start()

    loop(rank + 1, n_col, answer)
    loop(0, rank, lambda r: row_copy(col_of(r), col).wait_recv())
    fetches[4].wait()

    def multiply(pick, states, transposed):
        picked[...] = jnp.dot(pick[...], states[...], preferred_element_type=F32)
        for first in range(0, slots, 4):
            part = picked[first * nvec:(first + 4) * nvec].astype(BF16)
            none = jnp.zeros((2 * nvec, width), BF16)
            left = jnp.concatenate(
                [
                    jnp.concatenate([part[:2 * nvec], none], axis=1),
                    jnp.concatenate([none, part[2 * nvec:]], axis=1),
                ],
                axis=0,
            )
            b0, b1, b2, b3 = (held[first + index] for index in range(4))
            if transposed:
                right = jnp.concatenate(
                    [jnp.concatenate([b0, b1], axis=1), jnp.concatenate([b2, b3], axis=1)], axis=0
                )
                dims = (((1,), (0,)), ((), ()))
            else:
                right = jnp.concatenate(
                    [jnp.concatenate([b0, b2], axis=1), jnp.concatenate([b1, b3], axis=1)], axis=0
                )
                dims = (((1,), (1,)), ((), ()))
            both = lax.dot_general(left, right, dims, preferred_element_type=F32)
            for index in range(4):
                lanes = slice(index % 2 * width, (index % 2 + 1) * width)
                start = (first + index) * nvec
                terms[start:start + nvec] = both[index * nvec:(index + 1) * nvec, lanes]

    multiply(row_pick, row_st, True)
    low[...] = split_dot(col_place[...], terms[...])
    half = n_chip * piece
    theirs = pl.ds(pl.multiple_of((1 - core) * half, half), half)
    ours = pl.ds(pl.multiple_of(core * half, half), half)
    swap = pltpu.make_async_remote_copy(
        low.at[theirs], low_sib, sib_send.at[0], sib_recv.at[0], device_id=sibling, device_id_type=MESH
    )

    @pl.when(core == 1)
    def _():
        pl.semaphore_wait(sib_ready, 1)

    swap.start()
    swap.wait_recv()
    low_sib[...] += low[ours]

    def low_copy(source, target):
        return pltpu.make_async_remote_copy(
            low_sib.at[pieces(target)], low_in.at[pieces(source)], low_send.at[target], low_recv.at[source],
            device_id={"row": target * 2 + core, "col": col}, device_id_type=MESH,
        )

    def pass_low(q):
        col_copy(q, chip).wait_recv()
        low_copy(chip, q).start()

    loop(chip + 1, n_chip, pass_low)
    relay = pltpu.make_async_remote_copy(
        col_st.at[ours], col_st.at[ours], sib_send.at[1], sib_recv.at[1], device_id=sibling, device_id_type=MESH
    )
    relay.start()
    relay.wait_recv()

    multiply(col_pick, col_st, False)
    up[...] = split_dot(row_place[...], terms[...])

    def far_first(index):
        return (col + n_y + index // 2 * (2 * (index % 2) - 1)) % n_col

    def up_copy(source, target):
        return pltpu.make_async_remote_copy(
            up.at[pieces(target)], up_in.at[pieces(source)], up_send.at[target], up_recv.at[source],
            device_id={"row": row, "col": target}, device_id_type=MESH,
        )

    loop(1, n_col, lambda index: up_copy(col, far_first(index)).start())

    def add_low(source, total):
        low_copy(source, chip).wait_recv()
        return total + low_in[pieces(source)]

    def add_up(index, total):
        source = (col + index) % n_col
        up_copy(source, col).wait_recv()
        return total + up_in[pieces(source)]

    total = low_sib[pieces(chip)] + up[pieces(col)]
    total = lax.fori_loop(0, chip, add_low, total)
    total = lax.fori_loop(1, n_col, add_up, total)
    out[:, :width] = total[:nvec]
    out[:, width:] = total[nvec:]

    loop(1, n_col, lambda index: row_copy(col, (col + index) % n_col).wait_send())
    loop(0, chip, lambda q: col_copy(chip, q).wait_send())
    swap.wait_send()
    relay.wait_send()
    loop(chip + 1, n_chip, lambda q: low_copy(chip, q).wait_send())
    loop(1, n_col, lambda index: up_copy(col, (col + index) % n_col).wait_send())


def solution(mesh):
    n_row, n_col = mesh.shape["row"], mesh.shape["col"]
    n_chip = n_row // 2

    def local(vectors, blocks, row_index, col_index, live):
        nvec, piece_width = vectors.shape
        slots, width = blocks.shape[2], blocks.shape[4]
        rows, row_count, col_count = slots * nvec, 2 * n_col * nvec, 2 * n_row * nvec
        dma = lambda n: pltpu.SemaphoreType.DMA((n,))
        return pl.pallas_call(
            functools.partial(kernel, n_chip, n_col),
            out_shape=jax.ShapeDtypeStruct((nvec, piece_width), F32),
            in_specs=[pl.BlockSpec(memory_space=pltpu.MemorySpace.HBM)] * 5,
            out_specs=pl.BlockSpec(memory_space=pltpu.VMEM),
            scratch_shapes=[
                pltpu.VMEM(vectors.shape, BF16),
                pltpu.VMEM(row_index.shape, jnp.int32),
                pltpu.VMEM(col_index.shape, jnp.int32),
                pltpu.VMEM(live.shape, jnp.int32),
                pltpu.VMEM((slots, width, width), BF16),
                pltpu.VMEM((row_count, width), BF16),
                pltpu.VMEM((col_count, width), BF16),
                pltpu.VMEM((rows, row_count), BF16),
                pltpu.VMEM((rows, col_count), BF16),
                pltpu.VMEM((row_count, rows), BF16),
                pltpu.VMEM((col_count, rows), BF16),
                pltpu.VMEM((rows, width), F32),
                pltpu.VMEM((rows, width), F32),
                pltpu.VMEM((col_count, width), F32),
                pltpu.VMEM((col_count // 2, width), F32),
                pltpu.VMEM((col_count // 2, width), F32),
                pltpu.VMEM((row_count, width), F32),
                pltpu.VMEM((row_count, width), F32),
                dma(5),
                dma(n_col), dma(n_col), dma(n_chip), dma(n_chip), dma(n_chip), dma(n_chip), dma(n_col), dma(n_col),
                dma(2), dma(2),
                pltpu.SemaphoreType.REGULAR,
            ],
            compiler_params=pltpu.CompilerParams(
                collective_id=0, has_side_effects=True, vmem_limit_bytes=60 * 1024 * 1024
            ),
        )(vectors, blocks, row_index, col_index, live)

    return jax.shard_map(
        local,
        mesh=mesh,
        in_specs=(
            P(None, ("row", "col")),
            P("row", "col", None, None, None),
            P("row", "col", None),
            P("row", "col", None),
            P("row", "col"),
        ),
        out_specs=P(None, ("row", "col")),
        check_vma=False,
    )
```

time: 1860 us -> 36.6 us (0.02)
  waiting for transfers between devices: 1820 us -> 0 us
  Pallas kernels: 0 us -> 34.4 us
    all_gather x1 -> x0, waiting for transfers between devices: 1590 us -> none  [local(): every = lax.all_gather(vectors, ('row', 'col'), axis=1, tiled=True)]
    reduce_scatter x2 -> x0, waiting for transfers between devices: 237 us -> none  [the longest x1 179 us: local(): lax.psum_scatter(lower_part, 'row', scatter_dimension=1, tiled=True)]
    pallas_call x0 -> x1, Pallas kernels: none -> 34.4 us  [local(): pl.pallas_call(functools.partial(kernel, n_chip, n_col), out_shape=jax.Sh...]
  transfers between devices with their start and end apart: 3 -> 0, of which waited for: 3 -> 0; matrix products, arithmetic and copies ran while one was open for 0% -> 0% of each run, Pallas kernels for 0% -> 0%
where the time goes in v1:
time: 36.6 us; the launch traced here: 36.4 us
  Pallas kernels  34.4 us (94%)
  local copies, waits for them, and re-layouts  1.3 us (4%)
  between operations  0.66 us (2%)
    pallas_call x1, Pallas kernels, local(): pl.pallas_call(functools.partial(kernel, n_chip, n_col), out_shape=jax.Sh...  34.4 us
    unnamed x1, local copies, waits for them, and re-layouts  1.3 us

profile of v1, /device:TPU:1, one launch (start us, length us, event | category | flops | bytes accessed | tf_op | source)
XLA Modules:
  0.0 36.4 jit_solution(1158025832921867750)
XLA Ops:
  0.7 34.4 %shard_map.55 = f32[8,256]{1,0:T(8,128)} custom-call(bf16[8,256]{1,0:T(8,128)(2,1)} %vec_hbm.1, bf16[1,1,32,128,128]{4,3,2,1,0:T(8,128)(2,1)} %blocks.1, s32[1,1,32]{2,1,0:T(1,128)} %row_hbm.1, s32[1,1,32]{2,1,0:T(1,128)} %col_hbm.1, s32[1,1]{1,0:T(1,128)S(6)} %copy.7.live_hbm), custom_call_target="tpu_custom_call" | custom-call | tf_op jit(solution)/shard_map/pallas_call | solution.py:265
  35.1 1.3 %copy.8 = f32[8,256]{1,0:T(8,128)} copy(f32[8,256]{1,0:T(8,128)} %shard_map.55) | data formatting | bytes 16384

commit v2 on v1

--- a/solution.py
+++ b/solution.py
@@ -31,11 +31,10 @@
 
 
 def kernel(
-    n_chip, n_col, vec_hbm, blocks, row_hbm, col_hbm, live_hbm, out,
-    vec, row_index, col_index, live, held, row_st, col_st, row_pick, col_pick, row_place, col_place,
+    n_chip, n_col, vec, blocks, row_index, col_index, live, out,
+    held, row_st, col_st, row_pick, col_pick, row_place, col_place,
     picked, terms, low, low_sib, low_in, up, up_in,
-    fetch_sem, row_send, row_recv, col_send, col_recv, low_send, low_recv, up_send, up_recv, sib_send, sib_recv,
-    sib_ready,
+    fetch_sem, row_send, row_recv, chip_send, chip_recv, up_send, up_recv, sib_send, sib_recv, sib_ready,
 ):
     slots, width = held.shape[0], held.shape[1]
     nvec = vec.shape[0]
@@ -48,24 +47,15 @@
 
     turn = jnp.where(row == 0, 1, 0)
 
+    def swap_y(place):
+        return jnp.where(place < n_col // 2, place, n_col + 2 * (n_y // 2) - 2 - place // 2 * 2 + place % 2)
+
     def col_of(rank):
-        place = (rank + turn) % n_col
-        key = place // 2
-        y = jnp.where(key % 2 == 0, key // 2, n_y - (key + 1) // 2)
-        return y * 2 + place % 2
-
-    y = col // 2
-    key = jnp.where(2 * y < n_y + n_y % 2, 2 * y, 2 * (n_y - y) - 1)
-    rank = (key * 2 + col % 2 - turn + n_col) % n_col
-
-    fetches = [
-        pltpu.make_async_copy(source, target, fetch_sem.at[index])
-        for index, (source, target) in enumerate(
-            ((vec_hbm, vec), (row_hbm, row_index), (col_hbm, col_index), (live_hbm, live), (blocks.at[0, 0], held))
-        )
-    ]
-    for fetch in fetches:
-        fetch.start()
+        return swap_y((rank + turn) % n_col)
+
+    rank = (swap_y(col) + n_col - turn) % n_col
+
+    fetch = pltpu.make_async_copy(blocks.at[0, 0], held, fetch_sem)
 
     def pieces(slot):
         return pl.ds(pl.multiple_of(slot * piece, piece), piece)
@@ -78,14 +68,15 @@
     def greet(device):
         pl.semaphore_signal(barrier, inc=1, device_id=device, device_id_type=MESH)
 
+    near = jnp.minimum(chip + 7, n_chip)
+    loop(chip + 1, near, lambda q: greet({"row": q * 2 + core, "col": col}))
     loop(rank + 1, n_col, lambda r: greet({"row": row, "col": col_of(r)}))
-    loop(chip + 1, n_chip, lambda q: greet({"row": q * 2 + core, "col": col}))
+    loop(near, n_chip, lambda q: greet({"row": q * 2 + core, "col": col}))
 
     @pl.when(core == 1)
     def _():
         greet(sibling)
 
-    fetches[0].wait()
     own = vec[...].astype(F32)
     own = jnp.concatenate([own[:, :width], own[:, width:]], axis=0).astype(BF16)
     col_st[pieces(mine)] = own
@@ -104,22 +95,21 @@
     def col_copy(source, target):
         place = pieces(core * n_chip + source)
         return pltpu.make_async_remote_copy(
-            col_st.at[place], col_st.at[place], col_send.at[target], col_recv.at[source],
+            col_st.at[place], col_st.at[place], chip_send.at[target], chip_recv.at[source],
             device_id={"row": target * 2 + core, "col": col}, device_id_type=MESH,
         )
 
     def row_copy(source, target):
         return pltpu.make_async_remote_copy(
-            row_st.at[pieces(source)], row_st.at[pieces(source)], row_send.at[target], row_recv.at[source],
+            row_st.at[pieces(source)], row_st.at[pieces(source)], row_send, row_recv.at[source],
             device_id={"row": row, "col": target}, device_id_type=MESH,
         )
 
     loop(0, chip, lambda q: col_copy(chip, q).start())
     loop(0, rank, lambda r: row_copy(col, col_of(r)).start())
-
-    for fetch in fetches[1:4]:
-        fetch.wait()
-    alive = iota((1, slots), 1) < live[...]
+    fetch.start()
+
+    alive = iota((1, slots), 1) < live[0, 0]
     row_ids = jnp.where(alive, row_index[0], -1).astype(F32)
     col_ids = jnp.where(alive, col_index[0], -1).astype(F32)
     spread = (iota((slots, rows), 1) // nvec == iota((slots, rows), 0)).astype(F32).astype(BF16)
@@ -151,7 +141,7 @@
 
     loop(rank + 1, n_col, answer)
     loop(0, rank, lambda r: row_copy(col_of(r), col).wait_recv())
-    fetches[4].wait()
+    fetch.wait()
 
     def multiply(pick, states, transposed):
         picked[...] = jnp.dot(pick[...], states[...], preferred_element_type=F32)
@@ -201,7 +191,7 @@
 
     def low_copy(source, target):
         return pltpu.make_async_remote_copy(
-            low_sib.at[pieces(target)], low_in.at[pieces(source)], low_send.at[target], low_recv.at[source],
+            low_sib.at[pieces(target)], low_in.at[pieces(source)], chip_send.at[target], chip_recv.at[source],
             device_id={"row": target * 2 + core, "col": col}, device_id_type=MESH,
         )
 
@@ -209,48 +199,56 @@
         col_copy(q, chip).wait_recv()
         low_copy(chip, q).start()
 
-    loop(chip + 1, n_chip, pass_low)
+    late = n_chip // 2
+    first_late = jnp.maximum(chip + 1, late)
+    loop(chip + 1, late, pass_low)
+    loop(first_late, n_chip, lambda q: col_copy(q, chip).wait_recv())
     relay = pltpu.make_async_remote_copy(
         col_st.at[ours], col_st.at[ours], sib_send.at[1], sib_recv.at[1], device_id=sibling, device_id_type=MESH
     )
     relay.start()
+    loop(first_late, n_chip, lambda q: low_copy(chip, q).start())
     relay.wait_recv()
 
     multiply(col_pick, col_st, False)
     up[...] = split_dot(row_place[...], terms[...])
 
-    def far_first(index):
-        return (col + n_y + index // 2 * (2 * (index % 2) - 1)) % n_col
-
     def up_copy(source, target):
         return pltpu.make_async_remote_copy(
-            up.at[pieces(target)], up_in.at[pieces(source)], up_send.at[target], up_recv.at[source],
+            up.at[pieces(target)], up_in.at[pieces(source)], up_send, up_recv,
             device_id={"row": row, "col": target}, device_id_type=MESH,
         )
 
-    loop(1, n_col, lambda index: up_copy(col, far_first(index)).start())
+    loop(0, rank, lambda r: up_copy(col, col_of(r)).start())
+    loop(rank + 1, n_col, lambda r: up_copy(col, col_of(r)).start())
 
     def add_low(source, total):
         low_copy(source, chip).wait_recv()
         return total + low_in[pieces(source)]
 
     def add_up(index, total):
-        source = (col + index) % n_col
-        up_copy(source, col).wait_recv()
-        return total + up_in[pieces(source)]
+        return total + up_in[pieces((col + index) % n_col)]
 
     total = low_sib[pieces(chip)] + up[pieces(col)]
     total = lax.fori_loop(0, chip, add_low, total)
+    every_up = up_in.at[pl.ds(0, (n_col - 1) * piece)]
+    every_up = pltpu.make_async_remote_copy(
+        every_up, every_up, up_send, up_recv, device_id=sibling, device_id_type=MESH
+    )
+    every_up.wait_recv()
     total = lax.fori_loop(1, n_col, add_up, total)
     out[:, :width] = total[:nvec]
     out[:, width:] = total[nvec:]
 
-    loop(1, n_col, lambda index: row_copy(col, (col + index) % n_col).wait_send())
+    every_row = row_st.at[pl.ds(0, (n_col - 1) * piece)]
+    pltpu.make_async_remote_copy(
+        every_row, every_row, row_send, row_send, device_id=sibling, device_id_type=MESH
+    ).wait_send()
     loop(0, chip, lambda q: col_copy(chip, q).wait_send())
     swap.wait_send()
     relay.wait_send()
     loop(chip + 1, n_chip, lambda q: low_copy(chip, q).wait_send())
-    loop(1, n_col, lambda index: up_copy(col, (col + index) % n_col).wait_send())
+    every_up.wait_send()
 
 
 def solution(mesh):
@@ -261,17 +259,15 @@
         nvec, piece_width = vectors.shape
         slots, width = blocks.shape[2], blocks.shape[4]
         rows, row_count, col_count = slots * nvec, 2 * n_col * nvec, 2 * n_row * nvec
+        vmem, smem = pl.BlockSpec(memory_space=pltpu.VMEM), pl.BlockSpec(memory_space=pltpu.SMEM)
+        one = pltpu.SemaphoreType.DMA
         dma = lambda n: pltpu.SemaphoreType.DMA((n,))
         return pl.pallas_call(
             functools.partial(kernel, n_chip, n_col),
             out_shape=jax.ShapeDtypeStruct((nvec, piece_width), F32),
-            in_specs=[pl.BlockSpec(memory_space=pltpu.MemorySpace.HBM)] * 5,
-            out_specs=pl.BlockSpec(memory_space=pltpu.VMEM),
+            in_specs=[vmem, pl.BlockSpec(memory_space=pltpu.MemorySpace.HBM), vmem, vmem, smem],
+            out_specs=vmem,
             scratch_shapes=[
-                pltpu.VMEM(vectors.shape, BF16),
-                pltpu.VMEM(row_index.shape, jnp.int32),
-                pltpu.VMEM(col_index.shape, jnp.int32),
-                pltpu.VMEM(live.shape, jnp.int32),
                 pltpu.VMEM((slots, width, width), BF16),
                 pltpu.VMEM((row_count, width), BF16),
                 pltpu.VMEM((col_count, width), BF16),
@@ -286,13 +282,12 @@
                 pltpu.VMEM((col_count // 2, width), F32),
                 pltpu.VMEM((row_count, width), F32),
                 pltpu.VMEM((row_count, width), F32),
-                dma(5),
-                dma(n_col), dma(n_col), dma(n_chip), dma(n_chip), dma(n_chip), dma(n_chip), dma(n_col), dma(n_col),
-                dma(2), dma(2),
+                one,
+                one, dma(n_col), dma(n_chip), dma(n_chip), one, one, dma(2), dma(2),
                 pltpu.SemaphoreType.REGULAR,
             ],
             compiler_params=pltpu.CompilerParams(
-                collective_id=0, has_side_effects=True, vmem_limit_bytes=60 * 1024 * 1024
+                collective_id=0, has_side_effects=True, vmem_limit_bytes=53 * 1024 * 1024
             ),
         )(vectors, blocks, row_index, col_index, live)
 

time: 36.6 us -> 34.4 us (0.940)
  Pallas kernels: 34.4 us -> 32.2 us
    pallas_call x1, Pallas kernels: 34.4 us -> 32.2 us  [local(): pl.pallas_call(functools.partial(kernel, n_chip, n_col), out_shape=jax.Sh...]
    unnamed x1 -> x7, local copies, waits for them, and re-layouts: 1.3 us -> 1.29 us
where the time goes in v2:
time: 34.4 us; the launch traced here: 34.2 us
  Pallas kernels  32.2 us (94%)
  local copies, waits for them, and re-layouts  1.29 us (4%)
  between operations  0.71 us (2%)
    pallas_call x1, Pallas kernels, local(): pl.pallas_call(functools.partial(kernel, n_chip, n_col), out_shape=jax.Sh...  32.2 us
    unnamed x7, local copies, waits for them, and re-layouts  1.29 us

profile of v2, /device:TPU:1, one launch (start us, length us, event | category | flops | bytes accessed | tf_op | source)
XLA Modules:
  0.0 34.2 jit_solution(10077150665185970959)
XLA Ops:
  0.0 0.0 copy-start.2
  0.0 0.0 copy-start.1
  0.7 0.0 copy-done.2
  0.7 0.0 copy-done.1
  0.7 0.0 copy-start
  0.7 0.7 %copy-done = bf16[8,256]{1,0:T(8,128)(2,1)S(1)} copy-done((bf16[8,256]{1,0:T(8,128)(2,1)S(1)}, bf16[8,256]{1,0:T(8,128)(2,1)}, u32[]{:S(2)}) %copy-start) | copy-done | bytes 4120
  1.4 32.2 %shard_map.55 = f32[8,256]{1,0:T(8,128)S(1)} custom-call(bf16[8,256]{1,0:T(8,128)(2,1)S(1)} %copy-done, bf16[1,1,32,128,128]{4,3,2,1,0:T(8,128)(2,1)} %blocks.1, s32[1,1,32]{2,1,0:T(1,128)S(1)} %copy-done.1, s32[1,1,32]{2,1,0:T(1,128)S(1)} %copy-done.2, s32[1,1]{1,0:T(1,128)S(6)} %copy.7.live), custom_call_target="tpu_custom_call" | custom-call | tf_op jit(solution)/shard_map/pallas_call | solution.py:265
  33.6 0.6 %copy.8 = f32[8,256]{1,0:T(8,128)} copy(f32[8,256]{1,0:T(8,128)S(1)} %shard_map.55) | data formatting | bytes 16384
Async XLA Ops:
  0.0 0.7 %copy-start.2 = (s32[1,1,32]{2,1,0:T(1,128)S(1)}, s32[1,1,32]{2,1,0:T(1,128)}, u32[]{:S(2)}) copy-start(s32[1,1,32]{2,1,0:T(1,128)} %col_index.1) | copy-start | bytes 388
  0.0 0.7 %copy-start.1 = (s32[1,1,32]{2,1,0:T(1,128)S(1)}, s32[1,1,32]{2,1,0:T(1,128)}, u32[]{:S(2)}) copy-start(s32[1,1,32]{2,1,0:T(1,128)} %row_index.1) | copy-start | bytes 388
  0.7 0.7 %copy-start = (bf16[8,256]{1,0:T(8,128)(2,1)S(1)}, bf16[8,256]{1,0:T(8,128)(2,1)}, u32[]{:S(2)}) copy-start(bf16[8,256]{1,0:T(8,128)(2,1)} %vec.1) | copy-start | bytes 12292

commit v3 on v2

--- a/solution.py
+++ b/solution.py
@@ -34,7 +34,7 @@
     n_chip, n_col, vec, blocks, row_index, col_index, live, out,
     held, row_st, col_st, row_pick, col_pick, row_place, col_place,
     picked, terms, low, low_sib, low_in, up, up_in,
-    fetch_sem, row_send, row_recv, chip_send, chip_recv, up_send, up_recv, sib_send, sib_recv, sib_ready,
+    fetch_sem, row_send, row_recv, chip_send, chip_recv, up_send, up_recv, cross_send, cross_recv, sib_send, sib_recv, sib_ready,
 ):
     slots, width = held.shape[0], held.shape[1]
     nvec = vec.shape[0]
@@ -61,7 +61,12 @@
         return pl.ds(pl.multiple_of(slot * piece, piece), piece)
 
     col_st[...] = jnp.zeros_like(col_st)
-    mine = core * n_chip + chip
+    late = n_chip // 2
+
+    def spot(owner, source):
+        return source // late * n_chip + owner * late + source % late
+
+    mine = spot(core, chip)
 
     barrier = pltpu.get_barrier_semaphore()
 
@@ -73,6 +78,12 @@
     loop(rank + 1, n_col, lambda r: greet({"row": row, "col": col_of(r)}))
     loop(near, n_chip, lambda q: greet({"row": q * 2 + core, "col": col}))
 
+    hurried = chip == 0
+
+    @pl.when(hurried)
+    def _():
+        loop(late, n_chip, lambda q: greet({"row": q * 2 + 1 - core, "col": col}))
+
     @pl.when(core == 1)
     def _():
         greet(sibling)
@@ -82,7 +93,7 @@
     col_st[pieces(mine)] = own
     row_st[pieces(col)] = own
 
-    earlier = rank + chip + 1 - core
+    earlier = rank + chip + 1 - core + jnp.where(chip >= late, 1, 0)
 
     @pl.when(earlier > 0)
     def _():
@@ -93,7 +104,7 @@
         pl.semaphore_signal(sib_ready, inc=1, device_id=sibling, device_id_type=MESH)
 
     def col_copy(source, target):
-        place = pieces(core * n_chip + source)
+        place = pieces(spot(core, source))
         return pltpu.make_async_remote_copy(
             col_st.at[place], col_st.at[place], chip_send.at[target], chip_recv.at[source],
             device_id={"row": target * 2 + core, "col": col}, device_id_type=MESH,
@@ -105,7 +116,20 @@
             device_id={"row": row, "col": target}, device_id_type=MESH,
         )
 
-    loop(0, chip, lambda q: col_copy(chip, q).start())
+    def cross_copy(place):
+        return pltpu.make_async_remote_copy(
+            col_st.at[place], col_st.at[place], cross_send, cross_recv,
+            device_id={"row": 1 - core, "col": col}, device_id_type=MESH,
+        )
+
+    ahead = jnp.minimum(chip, 6)
+    loop(0, ahead, lambda q: col_copy(chip, q).start())
+
+    @pl.when(chip >= late)
+    def _():
+        cross_copy(pieces(mine)).start()
+
+    loop(ahead, chip, lambda q: col_copy(chip, q).start())
     loop(0, rank, lambda r: row_copy(col, col_of(r)).start())
     fetch.start()
 
@@ -122,16 +146,20 @@
         place = (ids // 2) % 2 * n_chip + ids // 4
         return jnp.where(ids < 0, -1, place * piece + ids % 2 * nvec + vector)
 
-    for ids, target, pick, place in (
-        (row_ids, row_target, row_pick, row_place),
-        (col_ids, col_target, col_pick, col_place),
+    def spot_target(ids, vector):
+        place = spot((ids // 2) % 2, ids // 4)
+        return jnp.where(ids < 0, -1, place * piece + ids % 2 * nvec + vector)
+
+    for ids, target, source, pick, place in (
+        (row_ids, row_target, row_target, row_pick, row_place),
+        (col_ids, col_target, spot_target, col_pick, col_place),
     ):
         count = place.shape[0]
         lane = jnp.dot(ids.astype(BF16), spread, preferred_element_type=F32).astype(jnp.int32)
         lane = target(lane, iota((1, rows), 1) % nvec)
         place[...] = (iota((count, rows), 0) == lane).astype(F32).astype(BF16)
         line = jnp.sum(spread_t * ids, axis=1, keepdims=True).astype(jnp.int32)
-        line = target(line, iota((rows, 1), 0) % nvec)
+        line = source(line, iota((rows, 1), 0) % nvec)
         pick[...] = (iota((rows, count), 1) == line).astype(F32).astype(BF16)
 
     def answer(r):
@@ -143,8 +171,7 @@
     loop(0, rank, lambda r: row_copy(col_of(r), col).wait_recv())
     fetch.wait()
 
-    def multiply(pick, states, transposed):
-        picked[...] = jnp.dot(pick[...], states[...], preferred_element_type=F32)
+    def multiply():
         for first in range(0, slots, 4):
             part = picked[first * nvec:(first + 4) * nvec].astype(BF16)
             none = jnp.zeros((2 * nvec, width), BF16)
@@ -156,23 +183,17 @@
                 axis=0,
             )
             b0, b1, b2, b3 = (held[first + index] for index in range(4))
-            if transposed:
-                right = jnp.concatenate(
-                    [jnp.concatenate([b0, b1], axis=1), jnp.concatenate([b2, b3], axis=1)], axis=0
-                )
-                dims = (((1,), (0,)), ((), ()))
-            else:
-                right = jnp.concatenate(
-                    [jnp.concatenate([b0, b2], axis=1), jnp.concatenate([b1, b3], axis=1)], axis=0
-                )
-                dims = (((1,), (1,)), ((), ()))
-            both = lax.dot_general(left, right, dims, preferred_element_type=F32)
+            right = jnp.concatenate(
+                [jnp.concatenate([b0, b1], axis=1), jnp.concatenate([b2, b3], axis=1)], axis=0
+            )
+            both = jnp.dot(left, right, preferred_element_type=F32)
             for index in range(4):
                 lanes = slice(index % 2 * width, (index % 2 + 1) * width)
                 start = (first + index) * nvec
                 terms[start:start + nvec] = both[index * nvec:(index + 1) * nvec, lanes]
 
-    multiply(row_pick, row_st, True)
+    picked[...] = jnp.dot(row_pick[...], row_st[...], preferred_element_type=F32)
+    multiply()
     low[...] = split_dot(col_place[...], terms[...])
     half = n_chip * piece
     theirs = pl.ds(pl.multiple_of((1 - core) * half, half), half)
@@ -186,8 +207,10 @@
         pl.semaphore_wait(sib_ready, 1)
 
     swap.start()
-    swap.wait_recv()
-    low_sib[...] += low[ours]
+
+    def take_low():
+        swap.wait_recv()
+        low_sib[...] += low[ours]
 
     def low_copy(source, target):
         return pltpu.make_async_remote_copy(
@@ -199,18 +222,53 @@
         col_copy(q, chip).wait_recv()
         low_copy(chip, q).start()
 
-    late = n_chip // 2
     first_late = jnp.maximum(chip + 1, late)
-    loop(chip + 1, late, pass_low)
+
+    @pl.when(hurried)
+    def _():
+        loop(chip + 1, late, lambda q: col_copy(q, chip).wait_recv())
+
+    @pl.when(jnp.logical_not(hurried))
+    def _():
+        take_low()
+        loop(chip + 1, late, pass_low)
+
+    quarter = late * piece
+
+    def relay(group):
+        place = pl.ds(pl.multiple_of(group * half + core * quarter, quarter), quarter)
+        return pltpu.make_async_remote_copy(
+            col_st.at[place], col_st.at[place], sib_send.at[1 + group], sib_recv.at[1 + group],
+            device_id=sibling, device_id_type=MESH,
+        )
+
+    @pl.when(chip < late)
+    def _():
+        relay(0).start()
+
+    for slot in range(slots):
+        held[slot] = held[slot].T
+
+    @pl.when(chip < late)
+    def _():
+        relay(0).wait_recv()
+
+    picked[...] = jnp.dot(col_pick[:, :half], col_st[:half], preferred_element_type=F32)
     loop(first_late, n_chip, lambda q: col_copy(q, chip).wait_recv())
-    relay = pltpu.make_async_remote_copy(
-        col_st.at[ours], col_st.at[ours], sib_send.at[1], sib_recv.at[1], device_id=sibling, device_id_type=MESH
-    )
-    relay.start()
-    loop(first_late, n_chip, lambda q: low_copy(chip, q).start())
-    relay.wait_recv()
-
-    multiply(col_pick, col_st, False)
+    every_late = pl.ds(0, (n_chip - late) * piece)
+
+    @pl.when(hurried)
+    def _():
+        cross_copy(every_late).wait_recv()
+
+    @pl.when(jnp.logical_not(hurried))
+    def _():
+        relay(1).start()
+        loop(first_late, n_chip, lambda q: low_copy(chip, q).start())
+        relay(1).wait_recv()
+
+    picked[...] += jnp.dot(col_pick[:, half:], col_st[half:], preferred_element_type=F32)
+    multiply()
     up[...] = split_dot(row_place[...], terms[...])
 
     def up_copy(source, target):
@@ -221,6 +279,11 @@
 
     loop(0, rank, lambda r: up_copy(col, col_of(r)).start())
     loop(rank + 1, n_col, lambda r: up_copy(col, col_of(r)).start())
+
+    @pl.when(hurried)
+    def _():
+        take_low()
+        loop(chip + 1, n_chip, lambda q: low_copy(chip, q).start())
 
     def add_low(source, total):
         low_copy(source, chip).wait_recv()
@@ -246,7 +309,19 @@
     ).wait_send()
     loop(0, chip, lambda q: col_copy(chip, q).wait_send())
     swap.wait_send()
-    relay.wait_send()
+
+    @pl.when(jnp.logical_not(hurried))
+    def _():
+        relay(1).wait_send()
+
+    @pl.when(chip >= late)
+    def _():
+        cross_copy(pieces(mine)).wait_send()
+
+    @pl.when(chip < late)
+    def _():
+        relay(0).wait_send()
+
     loop(chip + 1, n_chip, lambda q: low_copy(chip, q).wait_send())
     every_up.wait_send()
 
@@ -283,7 +358,7 @@
                 pltpu.VMEM((row_count, width), F32),
                 pltpu.VMEM((row_count, width), F32),
                 one,
-                one, dma(n_col), dma(n_chip), dma(n_chip), one, one, dma(2), dma(2),
+                one, dma(n_col), dma(n_chip), dma(n_chip), one, one, one, one, dma(3), dma(3),
                 pltpu.SemaphoreType.REGULAR,
             ],
             compiler_params=pltpu.CompilerParams(

time: 34.4 us -> 33.7 us (0.980)
  Pallas kernels: 32.2 us -> 31.4 us
    pallas_call x1, Pallas kernels: 32.2 us -> 31.4 us  [local(): pl.pallas_call(functools.partial(kernel, n_chip, n_col), out_shape=jax.Sh...]
where the time goes in v3:
time: 33.7 us; the launch traced here: 33.4 us
  Pallas kernels  31.4 us (93%)
  local copies, waits for them, and re-layouts  1.29 us (4%)
  between operations  0.71 us (2%)
    pallas_call x1, Pallas kernels, local(): pl.pallas_call(functools.partial(kernel, n_chip, n_col), out_shape=jax.Sh...  31.4 us
    unnamed x7, local copies, waits for them, and re-layouts  1.29 us

profile of v3, /device:TPU:1, one launch (start us, length us, event | category | flops | bytes accessed | tf_op | source)
XLA Modules:
  0.0 33.4 jit_solution(6025034082714645683)
XLA Ops:
  0.0 0.0 copy-start.2
  0.0 0.0 copy-start.1
  0.7 0.0 copy-done.2
  0.7 0.0 copy-done.1
  0.7 0.0 copy-start
  0.7 0.7 %copy-done = bf16[8,256]{1,0:T(8,128)(2,1)S(1)} copy-done((bf16[8,256]{1,0:T(8,128)(2,1)S(1)}, bf16[8,256]{1,0:T(8,128)(2,1)}, u32[]{:S(2)}) %copy-start) | copy-done | bytes 4120
  1.4 31.4 %shard_map.55 = f32[8,256]{1,0:T(8,128)S(1)} custom-call(bf16[8,256]{1,0:T(8,128)(2,1)S(1)} %copy-done, bf16[1,1,32,128,128]{4,3,2,1,0:T(8,128)(2,1)} %blocks.1, s32[1,1,32]{2,1,0:T(1,128)S(1)} %copy-done.1, s32[1,1,32]{2,1,0:T(1,128)S(1)} %copy-done.2, s32[1,1]{1,0:T(1,128)S(6)} %copy.7.live), custom_call_target="tpu_custom_call" | custom-call | tf_op jit(solution)/shard_map/pallas_call | solution.py:340
  32.8 0.6 %copy.8 = f32[8,256]{1,0:T(8,128)} copy(f32[8,256]{1,0:T(8,128)S(1)} %shard_map.55) | data formatting | bytes 16384
Async XLA Ops:
  0.0 0.7 %copy-start.2 = (s32[1,1,32]{2,1,0:T(1,128)S(1)}, s32[1,1,32]{2,1,0:T(1,128)}, u32[]{:S(2)}) copy-start(s32[1,1,32]{2,1,0:T(1,128)} %col_index.1) | copy-start | bytes 388
  0.0 0.7 %copy-start.1 = (s32[1,1,32]{2,1,0:T(1,128)S(1)}, s32[1,1,32]{2,1,0:T(1,128)}, u32[]{:S(2)}) copy-start(s32[1,1,32]{2,1,0:T(1,128)} %row_index.1) | copy-start | bytes 388
  0.7 0.7 %copy-start = (bf16[8,256]{1,0:T(8,128)(2,1)S(1)}, bf16[8,256]{1,0:T(8,128)(2,1)}, u32[]{:S(2)}) copy-start(bf16[8,256]{1,0:T(8,128)(2,1)} %vec.1) | copy-start | bytes 12292

commit v4 on v3

--- a/solution.py
+++ b/solution.py
@@ -289,20 +289,13 @@
         low_copy(source, chip).wait_recv()
         return total + low_in[pieces(source)]
 
-    def add_up(index, total):
-        return total + up_in[pieces((col + index) % n_col)]
-
-    total = low_sib[pieces(chip)] + up[pieces(col)]
+    up_in[pieces(col)] = up[pieces(col)]
+    total = low_sib[pieces(chip)]
     total = lax.fori_loop(0, chip, add_low, total)
     every_up = up_in.at[pl.ds(0, (n_col - 1) * piece)]
     every_up = pltpu.make_async_remote_copy(
         every_up, every_up, up_send, up_recv, device_id=sibling, device_id_type=MESH
     )
-    every_up.wait_recv()
-    total = lax.fori_loop(1, n_col, add_up, total)
-    out[:, :width] = total[:nvec]
-    out[:, width:] = total[nvec:]
-
     every_row = row_st.at[pl.ds(0, (n_col - 1) * piece)]
     pltpu.make_async_remote_copy(
         every_row, every_row, row_send, row_send, device_id=sibling, device_id_type=MESH
@@ -323,6 +316,11 @@
         relay(0).wait_send()
 
     loop(chip + 1, n_chip, lambda q: low_copy(chip, q).wait_send())
+    every_up.wait_recv()
+    for source in range(n_col):
+        total = total + up_in[source * piece:(source + 1) * piece]
+    out[:, :width] = total[:nvec]
+    out[:, width:] = total[nvec:]
     every_up.wait_send()
 
 

time: 33.7 us -> 33.5 us (level)
  no operation moved by 1% of the time
where the time goes in v4:
time: 33.5 us; the launch traced here: 33.2 us
  Pallas kernels  31.2 us (93%)
  local copies, waits for them, and re-layouts  1.29 us (4%)
  between operations  0.71 us (2%)
    pallas_call x1, Pallas kernels, local(): pl.pallas_call(functools.partial(kernel, n_chip, n_col), out_shape=jax.Sh...  31.2 us
    unnamed x7, local copies, waits for them, and re-layouts  1.29 us

profile of v4, /device:TPU:1, one launch (start us, length us, event | category | flops | bytes accessed | tf_op | source)
XLA Modules:
  0.0 33.2 jit_solution(15384798216863834556)
XLA Ops:
  0.0 0.0 copy-start.2
  0.0 0.0 copy-start.1
  0.7 0.0 copy-done.2
  0.7 0.0 copy-done.1
  0.7 0.0 copy-start
  0.7 0.7 %copy-done = bf16[8,256]{1,0:T(8,128)(2,1)S(1)} copy-done((bf16[8,256]{1,0:T(8,128)(2,1)S(1)}, bf16[8,256]{1,0:T(8,128)(2,1)}, u32[]{:S(2)}) %copy-start) | copy-done | bytes 4120
  1.4 31.2 %shard_map.55 = f32[8,256]{1,0:T(8,128)S(1)} custom-call(bf16[8,256]{1,0:T(8,128)(2,1)S(1)} %copy-done, bf16[1,1,32,128,128]{4,3,2,1,0:T(8,128)(2,1)} %blocks.1, s32[1,1,32]{2,1,0:T(1,128)S(1)} %copy-done.1, s32[1,1,32]{2,1,0:T(1,128)S(1)} %copy-done.2, s32[1,1]{1,0:T(1,128)S(6)} %copy.7.live), custom_call_target="tpu_custom_call" | custom-call | tf_op jit(solution)/shard_map/pallas_call | solution.py:338
  32.6 0.6 %copy.8 = f32[8,256]{1,0:T(8,128)} copy(f32[8,256]{1,0:T(8,128)S(1)} %shard_map.55) | data formatting | bytes 16384
Async XLA Ops:
  0.0 0.7 %copy-start.2 = (s32[1,1,32]{2,1,0:T(1,128)S(1)}, s32[1,1,32]{2,1,0:T(1,128)}, u32[]{:S(2)}) copy-start(s32[1,1,32]{2,1,0:T(1,128)} %col_index.1) | copy-start | bytes 388
  0.0 0.7 %copy-start.1 = (s32[1,1,32]{2,1,0:T(1,128)S(1)}, s32[1,1,32]{2,1,0:T(1,128)}, u32[]{:S(2)}) copy-start(s32[1,1,32]{2,1,0:T(1,128)} %row_index.1) | copy-start | bytes 388
  0.7 0.7 %copy-start = (bf16[8,256]{1,0:T(8,128)(2,1)S(1)}, bf16[8,256]{1,0:T(8,128)(2,1)}, u32[]{:S(2)}) copy-start(bf16[8,256]{1,0:T(8,128)(2,1)} %vec.1) | copy-start | bytes 12292
